TPU v7x, 32 devices: a whole 2x2x4 slice. The times are simulated.
32 devices in a mesh: group: 2 (over y), pool: 4 (over x, core), sub: 4 (over z).
Axes of the slice: x: 2, y: 2, z: 4, core: 2. Of those that a mesh axis runs over, the one named last changes fastest.
Arguments:
- hidden_in: bfloat16 [3, 128, 4096], P(None, ('group', 'pool', 'sub')), parts along dimension 1, may hold values from -6 to 6
- norm_gain: bfloat16 [4096], replicated, may hold values from 0.25 to 1.75
- expert_ids: int32 [3, 128, 8], P(None, ('group', 'pool', 'sub')), parts along dimension 1, may hold values from 0 to 31, all different within a row; in each aligned block of 4 rows (0 to 3, 4 to 7, ..., all dimensions but the last counted through in order) at most 2 rows name the same one
- gate_weights: bfloat16 [3, 128, 8], P(None, ('group', 'pool', 'sub')), parts along dimension 1, may hold values from 0.049804688 to 1
- w_gate: bfloat16 [32, 4096, 1536], P('pool', None, 'sub'), may hold values from -0.09375 to 0.09375
- w_up: bfloat16 [32, 4096, 1536], P('pool', None, 'sub'), may hold values from -0.09375 to 0.09375
- w_down: bfloat16 [32, 1536, 4096], P('pool', 'sub'), may hold values from -0.15625 to 0.15625
Outputs:
- layer_out: bfloat16 [3, 128, 4096], P(None, ('group', 'pool', 'sub')), parts along dimension 1
There are 2 independent parts, one for each index of `group`. A program takes and returns all parts, laid end to end along the dimension named above; an argument that names none is the same for every part. Nothing has to cross between parts.
Inputs may be any that keep to these rules, and one draw needn't show every extreme that they name: `expert_ids`: the 8 entries of a row differ. In each aligned block of 4 rows of one micro-batch (the rows of one device) no expert is named by more than 2 rows, a bound that some block reaches.
All inputs are finite; a program needn't handle non-finite values.
Results may differ from a plain program's by a relative error of at most 0.0095.
Values may be sent and summed in bfloat16 or wider, within the bound.
A program may use at most 192 MiB of HBM per device.

v0:
```python
import jax
import jax.numpy as jnp
from jax import lax
from jax.sharding import PartitionSpec as P


def rms_normed(hidden, norm_gain):
    values = hidden.astype(jnp.float32)
    scale = lax.rsqrt(jnp.mean(values * values, axis=-1, keepdims=True) + 1e-06)
    return (values * scale * norm_gain.astype(jnp.float32)).astype(jnp.bfloat16)


def dense_body(hidden_in, norm_gain, expert_ids, gate_weights, w_gate, w_up, w_down):
    batches, row_count, width = hidden_in.shape
    per_pool, _, hid = w_gate.shape
    pools = lax.axis_size("pool")
    own = batches * row_count
    normed = rms_normed(hidden_in, norm_gain).reshape(own, width)
    experts = jnp.arange(pools * per_pool, dtype=jnp.int32)
    gates = jnp.sum(
        jnp.where(expert_ids[..., None] == experts, gate_weights[..., None].astype(jnp.float32), 0.0), axis=2
    ).astype(jnp.bfloat16).reshape(own, pools * per_pool)
    rows = lax.all_gather(normed, ("pool", "sub"), axis=0, tiled=True)
    gates = lax.all_gather(gates, ("pool", "sub"), axis=0, tiled=True)
    gates = lax.dynamic_slice_in_dim(gates, lax.axis_index("pool") * per_pool, per_pool, axis=1)
    acts = []
    for e in range(per_pool):
        gate_act = jnp.dot(rows, w_gate[e], preferred_element_type=jnp.float32)
        up_act = jnp.dot(rows, w_up[e], preferred_element_type=jnp.float32)
        weight = gates[:, e : e + 1].astype(jnp.float32)
        acts.append((jax.nn.silu(gate_act) * up_act * weight).astype(jnp.bfloat16))
    act = jnp.concatenate(acts, axis=1)
    partial = jnp.dot(act, w_down.reshape(per_pool * hid, width), preferred_element_type=jnp.float32)
    summed = lax.psum_scatter(partial.astype(jnp.bfloat16), ("pool", "sub"), scatter_dimension=0, tiled=True)
    result = hidden_in.reshape(own, width).astype(jnp.float32) + summed.astype(jnp.float32)
    return result.astype(jnp.bfloat16).reshape(batches, row_count, width)


def solution(mesh):
    in_specs = (
        P(None, ("group", "pool", "sub"), None),
        P(),
        P(None, ("group", "pool", "sub"), None),
        P(None, ("group", "pool", "sub"), None),
        P("pool", None, "sub"),
        P("pool", None, "sub"),
        P("pool", "sub", None),
    )
    out_specs = P(None, ("group", "pool", "sub"), None)
    return jax.shard_map(dense_body, mesh=mesh, in_specs=in_specs, out_specs=out_specs, check_vma=False)
```

profile of v0, /device:TPU:0, one launch (start us, length us, event | category | flops | bytes accessed | tf_op | source)
XLA Modules:
  0.0 173.2 jit_solution(17070146078687421124)
XLA Ops:
  6.5 0.0 all-gather.4.cloned.1.call-start
  6.5 0.7 convert_element_type.70
  7.2 1.0 multiply_reduce_fusion
  8.3 1.0 multiply_convert_fusion
  9.3 0.7 reshape.39
  10.0 0.0 all-gather.4.cloned.1.call-update
  10.0 0.7 convert_element_type.72
  10.7 0.8 select_reduce_fusion
  11.5 34.7 %all-gather.1 = bf16[16,12,32]{2,1,0:T(8,128)(2,1)S(1)} all-gather(bf16[1,12,32]{2,1,0:T(8,128)(2,1)S(1)} %reshape.41), channel_id=1, replica_groups=mesh['group'=2,'pool'=4,'sub'=4] {'pool','sub'}, dimensions={0}, use_global_device_ids=true | all-gather | bytes 13056 | tf_op jit(solution)/shard_map/all_gather | solution.py:24
  46.2 0.4 convert_reduce_fusion
  46.6 7.8 %all-gather.4.cloned.1.call-done = bf16[16,12,4096]{2,1,0:T(8,128)(2,1)} async-done(((bf16[1,12,4096]{2,1,0:T(8,128)(2,1)}), bf16[16,12,4096]{2,1,0:T(8,128)(2,1)}) %all-gather.4.cloned.1.call-update) | async-done | bytes 1572880 | tf_op jit(solution)/shard_map/all_gather | solution.py:23
  54.4 2.5 %reshape.40 = bf16[192,4096]{1,0:T(8,128)(2,1)S(1)} reshape(bf16[16,12,4096]{2,1,0:T(8,128)(2,1)} %all-gather.4.cloned.1.call-done) | data formatting | bytes 3145728
  56.9 0.0 copy-start.2
  56.9 3.1 %fusion.31 = f32[192,384]{1,0:T(8,128)S(1)} fusion(bf16[192,4096]{1,0:T(8,128)(2,1)S(1)} %reshape.40, bf16[8,4096,384]{2,1,0:T(8,128)(2,1)} %param.11), kind=kOutput, calls=%fused_computation.31 | convolution fusion | flops 603979776 | bytes 5013504 | tf_op jit(solution)/shard_map/dot_general | solution.py:28
  60.0 3.6 %fusion.27 = f32[192,384]{1,0:T(8,128)S(1)} fusion(bf16[192,4096]{1,0:T(8,128)(2,1)S(1)} %reshape.40, bf16[8,4096,384]{2,1,0:T(8,128)(2,1)} %param.11), kind=kOutput, calls=%fused_computation.27 | convolution fusion | flops 603979776 | bytes 5013504 | tf_op jit(solution)/shard_map/dot_general | solution.py:28
  63.6 3.7 %fusion.23 = f32[192,384]{1,0:T(8,128)S(1)} fusion(bf16[192,4096]{1,0:T(8,128)(2,1)S(1)} %reshape.40, bf16[8,4096,384]{2,1,0:T(8,128)(2,1)} %param.11), kind=kOutput, calls=%fused_computation.23 | convolution fusion | flops 603979776 | bytes 5013504 | tf_op jit(solution)/shard_map/dot_general | solution.py:28
  67.2 2.9 %fusion.19 = f32[192,384]{1,0:T(8,128)S(1)} fusion(bf16[192,4096]{1,0:T(8,128)(2,1)S(1)} %reshape.40, bf16[8,4096,384]{2,1,0:T(8,128)(2,1)} %param.11), kind=kOutput, calls=%fused_computation.19 | convolution fusion | flops 603979776 | bytes 5013504 | tf_op jit(solution)/shard_map/dot_general | solution.py:28
  70.2 0.0 copy-done.2
  70.2 0.0 slice-start
  70.2 1.0 fusion.15
  71.2 0.0 slice-start.1
  71.2 1.0 fusion.11
  72.3 0.0 slice-start.2
  72.3 1.0 fusion.7
  73.3 0.0 slice-start.3
  73.3 1.0 fusion.3
  74.4 0.0 slice-start.4
  74.4 3.6 %fusion.121 = bf16[192,3072]{1,0:T(8,128)(2,1)S(1)} fusion(bf16[192,4096]{1,0:T(8,128)(2,1)S(1)} %reshape.40, bf16[8,4096,384]{2,1,0:T(8,128)(2,1)} %param.12, f32[192,384]{1,0:T(8,128)S(1)} %fusion.31, f32[192]{0:T(256)S(1)} %get-tuple-element.12), kind=kOutput, calls=%fused_computation.73 | convolution fusion | flops 604495872 | bytes 5161728 | tf_op jit(solution)/shard_map/dot_general | solution.py:29
  78.0 0.0 slice-start.5
  78.0 3.1 %fusion.124 = bf16[192,3072]{1,0:T(8,128)(2,1)S(1)} fusion(bf16[192,3072]{1,0:T(8,128)(2,1)S(1)} %fusion.121, bf16[192,4096]{1,0:T(8,128)(2,1)S(1)} %reshape.40, bf16[8,4096,384]{2,1,0:T(8,128)(2,1)} %param.12, f32[192,384]{1,0:T(8,128)S(1)} %fusion.27, f32[192]{0:T(256)S(1)} %get-tuple-element.11), kind=kOutput, calls=%fused_computation.74 | convolution fusion | flops 604495872 | bytes 5161984 | tf_op jit(solution)/shard_map/dot_general | solution.py:29
  81.1 0.0 slice-done
  81.1 0.0 slice-done.1
  81.1 0.0 slice-done.2
  81.1 0.0 slice-done.3
  81.1 0.0 slice-done.4
  81.1 0.1 slice-done.5
  81.2 1.0 fusion.127
  82.2 1.1 fusion.130
  83.3 1.3 fusion.133
  84.6 1.1 fusion.136
  85.6 1.1 fusion.139
  86.7 1.1 fusion.142
  87.8 11.0 %convolution_convert_fusion = bf16[192,4096]{1,0:T(8,128)(2,1)S(1)} fusion(bf16[192,3072]{1,0:T(8,128)(2,1)S(1)} %fusion.142, bf16[3072,4096]{1,0:T(8,128)(2,1)} %bitcast.136), kind=kOutput, calls=%fused_computation | convolution fusion | flops 4832624640 | bytes 27918336 | tf_op jit(solution)/shard_map/dot_general | solution.py:33
  98.8 0.0 copy-start
  98.8 0.0 copy-start.1
  98.8 52.5 %fusion = bf16[16,4096]{1,0:T(8,128)(2,1)S(1)} fusion(bf16[192,4096]{1,0:T(8,128)(2,1)S(1)} %convolution_convert_fusion), kind=kCustom, calls=%all-reduce-scatter | all-reduce-scatter fusion | flops 1048577 | bytes 1704448
  151.3 1.3 collective-permute-start
  152.6 2.2 %collective-permute-start.1 = (bf16[16,4096]{1,0:T(8,128)(2,1)S(1)}, bf16[16,4096]{1,0:T(8,128)(2,1)S(1)}, u32[]{:S(2)}, u32[]{:S(2)}) collective-permute-start(bf16[16,4096]{1,0:T(8,128)(2,1)S(1)} %fusion), channel_id=1, source_target_pairs={{0,2},{1,3},{2,4},{3,5},{4,6},{5,7},{6,8},{7,9},{8,10},{9,11},{10,... | collective-permute-start | bytes 393224
  154.9 4.2 %collective-permute-start.2 = (bf16[16,4096]{1,0:T(8,128)(2,1)S(1)}, bf16[16,4096]{1,0:T(8,128)(2,1)S(1)}, u32[]{:S(2)}, u32[]{:S(2)}) collective-permute-start(bf16[16,4096]{1,0:T(8,128)(2,1)S(1)} %fusion), channel_id=1, source_target_pairs={{0,3},{1,4},{2,5},{3,6},{4,7},{5,8},{6,9},{7,10},{8,11},{9,12},{10... | collective-permute-start | bytes 393224
  159.1 3.9 %collective-permute-start.3 = (bf16[12,4096]{1,0:T(8,128)(2,1)S(1)}, bf16[12,4096]{1,0:T(8,128)(2,1)S(1)}, u32[]{:S(2)}, u32[]{:S(2)}) collective-permute-start(bf16[12,4096]{1,0:T(8,128)(2,1)S(1)} %slice.96), channel_id=1, source_target_pairs={{0,4},{1,5},{2,6},{3,7},{4,8},{5,9},{6,10},{7,11},{8,12},{9,13},{1... | collective-permute-start | bytes 294920
  163.0 0.0 copy-done
  163.1 0.0 copy-done.1
  163.1 0.6 dynamic-slice.12
  164.3 0.0 collective-permute-done.3
  164.3 0.0 collective-permute-done
  164.3 0.0 collective-permute-done.1
  164.3 0.0 collective-permute-done.2
  164.3 1.2 concatenate.4
  165.6 0.1 add_convert_fusion
  165.6 0.7 reshape.29
  (6 shorter events, 0.1 us)
Async XLA Ops:
  6.5 47.9 %all-gather.4.cloned.1.call-start = ((), (), s32[]{:S(2)}) async-start(), calls=%async_computation | async-start | bytes 2228224 | tf_op jit(solution)/shard_map/all_gather | solution.py:23
  56.9 13.3 %copy-start.2 = (bf16[8,4096,384]{2,1,0:T(8,128)(2,1)S(1)}, bf16[8,4096,384]{2,1,0:T(8,128)(2,1)}, u32[]{:S(2)}) copy-start(bf16[8,4096,384]{2,1,0:T(8,128)(2,1)} %param.11) | copy-start | bytes 75497472
  70.2 10.9 %slice-start = ((s8[25165824]{0:T(1024)(128)(4,1)}), s8[4194304]{0:T(1024)(128)(4,1)S(1)}, s32[]{:S(2)}) async-start(s8[25165824]{0:T(1024)(128)(4,1)} %bitcast.134), calls=%async_computation.1 | async-start | bytes 8388608
  71.2 9.9 %slice-start.1 = ((s8[25165824]{0:T(1024)(128)(4,1)}), s8[4194304]{0:T(1024)(128)(4,1)S(1)}, s32[]{:S(2)}) async-start(s8[25165824]{0:T(1024)(128)(4,1)} %bitcast.134), calls=%async_computation.2 | async-start | bytes 8388608
  72.3 8.8 %slice-start.2 = ((s8[25165824]{0:T(1024)(128)(4,1)}), s8[4194304]{0:T(1024)(128)(4,1)S(1)}, s32[]{:S(2)}) async-start(s8[25165824]{0:T(1024)(128)(4,1)} %bitcast.134), calls=%async_computation.3 | async-start | bytes 8388608
  73.3 7.8 %slice-start.3 = ((s8[25165824]{0:T(1024)(128)(4,1)}), s8[4194304]{0:T(1024)(128)(4,1)S(1)}, s32[]{:S(2)}) async-start(s8[25165824]{0:T(1024)(128)(4,1)} %bitcast.134), calls=%async_computation.4 | async-start | bytes 8388608
  74.4 6.7 %slice-start.4 = ((s8[25165824]{0:T(1024)(128)(4,1)}), s8[4194304]{0:T(1024)(128)(4,1)S(1)}, s32[]{:S(2)}) async-start(s8[25165824]{0:T(1024)(128)(4,1)} %bitcast.134), calls=%async_computation.5 | async-start | bytes 8388608
  78.0 3.2 %slice-start.5 = ((s8[25165824]{0:T(1024)(128)(4,1)}), s8[4194304]{0:T(1024)(128)(4,1)S(1)}, s32[]{:S(2)}) async-start(s8[25165824]{0:T(1024)(128)(4,1)} %bitcast.134), calls=%async_computation.6 | async-start | bytes 8388608
  98.8 64.2 %copy-start = (bf16[3,4,4096]{2,1,0:T(4,128)(2,1)S(1)}, bf16[3,4,4096]{2,1,0:T(4,128)(2,1)}, u32[]{:S(2)}) copy-start(bf16[3,4,4096]{2,1,0:T(4,128)(2,1)} %param.7) | copy-start | bytes 294916
  98.8 64.2 %copy-start.1 = (u32[32]{0:T(128)S(1)}, u32[32]{0:T(128)}, u32[]{:S(2)}) copy-start(u32[32]{0:T(128)} %constant.33) | copy-start | bytes 388
  151.3 13.0 %collective-permute-start = (bf16[16,4096]{1,0:T(8,128)(2,1)S(1)}, bf16[16,4096]{1,0:T(8,128)(2,1)S(1)}, u32[]{:S(2)}, u32[]{:S(2)}) collective-permute-start(bf16[16,4096]{1,0:T(8,128)(2,1)S(1)} %fusion), channel_id=1, source_target_pairs={{0,1},{1,2},{2,3},{3,4},{4,5},{5,6},{6,7},{7,8},{8,9},{9,10},{10,1... | collective-permute-start | bytes 393224
  152.6 11.7 %collective-permute-start.1 = (bf16[16,4096]{1,0:T(8,128)(2,1)S(1)}, bf16[16,4096]{1,0:T(8,128)(2,1)S(1)}, u32[]{:S(2)}, u32[]{:S(2)}) collective-permute-start(bf16[16,4096]{1,0:T(8,128)(2,1)S(1)} %fusion), channel_id=1, source_target_pairs={{0,2},{1,3},{2,4},{3,5},{4,6},{5,7},{6,8},{7,9},{8,10},{9,11},{10,... | collective-permute-start | bytes 393224
  154.9 9.5 %collective-permute-start.2 = (bf16[16,4096]{1,0:T(8,128)(2,1)S(1)}, bf16[16,4096]{1,0:T(8,128)(2,1)S(1)}, u32[]{:S(2)}, u32[]{:S(2)}) collective-permute-start(bf16[16,4096]{1,0:T(8,128)(2,1)S(1)} %fusion), channel_id=1, source_target_pairs={{0,3},{1,4},{2,5},{3,6},{4,7},{5,8},{6,9},{7,10},{8,11},{9,12},{10... | collective-permute-start | bytes 393224
  159.1 5.2 %collective-permute-start.3 = (bf16[12,4096]{1,0:T(8,128)(2,1)S(1)}, bf16[12,4096]{1,0:T(8,128)(2,1)S(1)}, u32[]{:S(2)}, u32[]{:S(2)}) collective-permute-start(bf16[12,4096]{1,0:T(8,128)(2,1)S(1)} %slice.96), channel_id=1, source_target_pairs={{0,4},{1,5},{2,6},{3,7},{4,8},{5,9},{6,10},{7,11},{8,12},{9,13},{1... | collective-permute-start | bytes 294920
Sparse Core Ops, SparseCore 0:
  10.1 44.2 all-gather.3
where the time goes:
time: 176 us; the launch traced here: 173 us
  blocking collectives  87.1 us (49%)
  matrix products  41.6 us (24%)
  between operations  14.4 us (8%)
  starting transfers between devices  11.6 us (7%)
  waiting for transfers between devices  7.84 us (4%)
  local copies, waits for them, and re-layouts  5.87 us (3%)
  other arithmetic  4.68 us (3%)
    unnamed x1, blocking collectives  52.5 us
    all_gather x1, blocking collectives, dense_body(): gates = lax.all_gather(gates, ('pool', 'sub'), axis=0, tiled=True)  34.7 us
    dot_general x8, matrix products, dense_body(): gate_act = jnp.dot(rows, w_gate[e], preferred_element_type=jnp.float32)  17.4 us
    dot_general x8, matrix products, dense_body(): up_act = jnp.dot(rows, w_up[e], preferred_element_type=jnp.float32)  13.2 us
    unnamed x4, starting transfers between devices  11.6 us
    dot_general x1, matrix products, dense_body(): jnp.dot(act, w_down.reshape(per_pool * hid, width), preferred_element_typ...  11 us
    all_gather x1, waiting for transfers between devices, dense_body(): rows = lax.all_gather(normed, ('pool', 'sub'), axis=0, tiled=True)  7.81 us
    unnamed x25, local copies, waits for them, and re-layouts  5.16 us
  transfers between devices with their start and end apart: 5, of which 1 were waited for; matrix products, arithmetic and copies ran while one was open for 1% of the time, Pallas kernels for 0%

commit v1 on v0

--- a/solution.py
+++ b/solution.py
@@ -1,6 +1,10 @@
+import functools
+
 import jax
 import jax.numpy as jnp
 from jax import lax
+from jax.experimental import pallas as pl
+from jax.experimental.pallas import tpu as pltpu
 from jax.sharding import PartitionSpec as P
 
 
@@ -36,6 +40,314 @@
     return result.astype(jnp.bfloat16).reshape(batches, row_count, width)
 
 
+MESH = pl.DeviceIdType.MESH
+F32 = jnp.float32
+BF16 = jnp.bfloat16
+PAD = 16
+GW = 128
+KC = 4
+NC = 8
+SLOTS = 12
+
+
+def expert_kernel(
+    subs, hidden, gain, ids, gws, w_gate, w_up, w_down, out,
+    xg, acc, act, y, crecv, xsend, xrecv, zsend, zrecv, gu, wd, rowf, sumf,
+    gu_sem, wd_sem, az_s, az_r, ax_s, ax_r, ac_s, ac_r,
+    rc_s, rc_r, rx_s, rx_r, rz_s, rz_r,
+):
+    batches, rows, width = hidden.shape
+    per_pool, _, hid = w_gate.shape
+    kw, nw = width // KC, width // NC
+    group, pool, sub = lax.axis_index("group"), lax.axis_index("pool"), lax.axis_index("sub")
+    core, side = pool % 2, pool // 2
+    quad = subs * PAD
+    half = 2 * quad
+    xrow = core * half + side * quad
+    own = pl.multiple_of(xrow + sub * PAD, PAD)
+    peer_core = (group, side * 2 + 1 - core, sub)
+    peer_side = (group, (1 - side) * 2 + core, sub)
+    peer_sub = [(group, pool, (sub + d) % subs) for d in range(1, subs)]
+    steps = KC * per_pool
+
+    def gu_copies(step):
+        slot, e = step % SLOTS, step % per_pool
+        krow = pl.multiple_of(step // per_pool * kw, kw)
+        return (
+            pltpu.make_async_copy(w_gate.at[e, pl.ds(krow, kw), :], gu.at[slot, :, pl.ds(0, hid)], gu_sem.at[slot, 0]),
+            pltpu.make_async_copy(w_up.at[e, pl.ds(krow, kw), :], gu.at[slot, :, pl.ds(hid, hid)], gu_sem.at[slot, 1]),
+        )
+
+    def wd_copy(n):
+        return pltpu.make_async_copy(
+            w_down.at[:, :, pl.ds(pl.multiple_of(n * nw, nw), nw)], wd.at[n], wd_sem.at[n]
+        )
+
+    def first(step, carry):
+        for copy in gu_copies(step):
+            copy.start()
+        return carry
+
+    lax.fori_loop(0, SLOTS, first, 0)
+
+    barrier = pltpu.get_barrier_semaphore()
+    for peer in [peer_core, peer_side] + peer_sub:
+        pl.semaphore_signal(barrier, inc=1, device_id=peer, device_id_type=MESH)
+
+    rowf[...] = jnp.zeros_like(rowf)
+    lane = lax.broadcasted_iota(jnp.int32, (rows, GW), 1)
+    gain_row = gain[...].astype(F32)
+    for m in range(batches):
+        values = hidden[m].astype(F32)
+        scale = lax.rsqrt(jnp.mean(values * values, axis=-1, keepdims=True) + 1e-06)
+        rowf[rows * m : rows * (m + 1), GW:] = values * scale * gain_row
+        names, weights = ids[m], gws[m].astype(F32)
+        table = jnp.zeros((rows, GW), F32)
+        for k in range(names.shape[1]):
+            table = table + jnp.where(names[:, k : k + 1] == lane, weights[:, k : k + 1], 0.0)
+        rowf[rows * m : rows * (m + 1), :GW] = table
+    xg[pl.ds(own, PAD), :] = rowf[...].astype(BF16)
+
+    pl.semaphore_wait(barrier, subs + 1)
+
+    def cols(c):
+        return pl.ds(0, GW + kw) if c == 0 else pl.ds(GW + c * kw, kw)
+
+    def az(c, d):
+        ref = xg.at[pl.ds(own, PAD), cols(c)]
+        return pltpu.make_async_remote_copy(
+            ref, ref, az_s.at[c, d], az_r.at[c, d], device_id=peer_sub[d], device_id_type=MESH
+        )
+
+    def az_wait(c):
+        for d in range(subs - 1):
+            az(c, d).wait_recv()
+
+    def ax(c):
+        ref = xg.at[pl.ds(pl.multiple_of(xrow, PAD), quad), cols(c)]
+        return pltpu.make_async_remote_copy(
+            ref, ref, ax_s.at[c], ax_r.at[c], device_id=peer_side, device_id_type=MESH
+        )
+
+    def ac(c):
+        ref = xg.at[pl.ds(pl.multiple_of(core * half, PAD), half), cols(c)]
+        return pltpu.make_async_remote_copy(
+            ref, ref, ac_s.at[c], ac_r.at[c], device_id=peer_core, device_id_type=MESH
+        )
+
+    def relay_x(c):
+        az_wait(c)
+        ax(c).start()
+
+    def relay_c(c):
+        ax(c).wait_recv()
+        ac(c).start()
+
+    for c in range(KC):
+        for d in range(subs - 1):
+            az(c, d).start()
+    acc[...] = jnp.zeros_like(acc)
+    relay_x(0)
+    relay_x(1)
+    relay_c(0)
+
+    def gu_step(c, step, carry):
+        slot, e = step % SLOTS, step % per_pool
+        for copy in gu_copies(step):
+            copy.wait()
+        total = acc[e] + jnp.dot(
+            xg[:, GW + c * kw : GW + (c + 1) * kw], gu[slot], preferred_element_type=F32
+        )
+        if c < KC - 1:
+            acc[e] = total
+        else:
+            g, u = total[:, :hid], total[:, hid:]
+            lanes = lax.broadcasted_iota(jnp.int32, (2 * half, GW), 1)
+            weight = jnp.sum(
+                jnp.where(lanes == pool * per_pool + e, xg[:, :GW].astype(F32), 0.0), axis=1, keepdims=True
+            )
+            act[:, pl.ds(pl.multiple_of(e * hid, hid), hid)] = (
+                g / (1.0 + jnp.exp(-g)) * u * weight
+            ).astype(BF16)
+
+        @pl.when(step + SLOTS < steps)
+        def _():
+            for copy in gu_copies(step + SLOTS):
+                copy.start()
+
+        extra = step + SLOTS - steps
+
+        @pl.when((extra >= 0) & (extra < NC))
+        def _():
+            wd_copy(extra).start()
+
+        return carry
+
+    cut = per_pool // 2
+    for c in range(KC):
+        ac(c).wait_recv()
+        base = c * per_pool
+        lax.fori_loop(base, base + cut, functools.partial(gu_step, c), 0)
+        if c + 2 < KC:
+            relay_x(c + 2)
+        if c + 1 < KC:
+            relay_c(c + 1)
+        lax.fori_loop(base + cut, base + per_pool, functools.partial(gu_step, c), 0)
+
+    def ncols(n):
+        return pl.ds(pl.multiple_of(n * nw, nw), nw)
+
+    def rc(n):
+        return pltpu.make_async_remote_copy(
+            y.at[pl.ds(pl.multiple_of((1 - core) * half, PAD), half), ncols(n)], crecv.at[:, ncols(n)],
+            rc_s.at[n], rc_r.at[n], device_id=peer_core, device_id_type=MESH,
+        )
+
+    def rx(n):
+        return pltpu.make_async_remote_copy(
+            xsend.at[:, ncols(n)], xrecv.at[:, ncols(n)],
+            rx_s.at[n], rx_r.at[n], device_id=peer_side, device_id_type=MESH,
+        )
+
+    def rz(n, d):
+        row = pl.multiple_of((sub + d + 1) % subs * PAD, PAD)
+        return pltpu.make_async_remote_copy(
+            zsend.at[pl.ds(row, PAD), ncols(n)], zrecv.at[d, :, ncols(n)],
+            rz_s.at[n, d], rz_r.at[n, d], device_id=peer_sub[d], device_id_type=MESH,
+        )
+
+    def down_step(n, carry):
+        @pl.when(n < NC)
+        def _():
+            wd_copy(n).wait()
+            y[:, ncols(n)] = jnp.dot(
+                act[...], wd[n].reshape(per_pool * hid, nw), preferred_element_type=F32
+            ).astype(BF16)
+            rc(n).start()
+
+        @pl.when((n >= 1) & (n < NC + 1))
+        def _():
+            m = n - 1
+            rc(m).wait_recv()
+            far = pl.multiple_of((1 - side) * quad, PAD)
+            xsend[:, ncols(m)] = (
+                y[pl.ds(pl.multiple_of(core * half + (1 - side) * quad, PAD), quad), ncols(m)].astype(F32)
+                + crecv[pl.ds(far, quad), ncols(m)].astype(F32)
+            ).astype(BF16)
+            rx(m).start()
+
+        @pl.when((n >= 2) & (n < NC + 2))
+        def _():
+            m = n - 2
+            rx(m).wait_recv()
+            near = pl.multiple_of(side * quad, PAD)
+            zsend[:, ncols(m)] = (
+                y[pl.ds(pl.multiple_of(xrow, PAD), quad), ncols(m)].astype(F32)
+                + crecv[pl.ds(near, quad), ncols(m)].astype(F32)
+                + xrecv[:, ncols(m)].astype(F32)
+            ).astype(BF16)
+            for d in range(subs - 1):
+                rz(m, d).start()
+
+        @pl.when(n >= 3)
+        def _():
+            m = n - 3
+            total = zsend[pl.ds(pl.multiple_of(sub * PAD, PAD), PAD), ncols(m)].astype(F32)
+            for d in range(subs - 1):
+                rz(m, d).wait_recv()
+                total = total + zrecv[d, :, ncols(m)].astype(F32)
+            sumf[...] = total
+            for b in range(batches):
+                out[b, :, ncols(m)] = (
+                    hidden[b, :, ncols(m)].astype(F32) + sumf[rows * b : rows * (b + 1), :]
+                ).astype(BF16)
+
+        return carry
+
+    lax.fori_loop(0, NC + 3, down_step, 0)
+
+    for c in range(KC):
+        for d in range(subs - 1):
+            az(c, d).wait_send()
+        ax(c).wait_send()
+        ac(c).wait_send()
+
+    def sent(n, carry):
+        rc(n).wait_send()
+        rx(n).wait_send()
+        for d in range(subs - 1):
+            rz(n, d).wait_send()
+        return carry
+
+    lax.fori_loop(0, NC, sent, 0)
+
+
+def kernel_body(hidden_in, norm_gain, expert_ids, gate_weights, w_gate, w_up, w_down):
+    batches, rows, width = hidden_in.shape
+    per_pool, _, hid = w_gate.shape
+    subs = lax.axis_size("sub")
+    total = 4 * subs * PAD
+    vmem = pl.BlockSpec(memory_space=pltpu.VMEM)
+    hbm = pl.BlockSpec(memory_space=pl.ANY)
+    dma = pltpu.SemaphoreType.DMA
+    others = subs - 1
+    return pl.pallas_call(
+        functools.partial(expert_kernel, subs),
+        out_shape=jax.ShapeDtypeStruct(hidden_in.shape, BF16),
+        in_specs=[vmem] * 4 + [hbm] * 3,
+        out_specs=vmem,
+        scratch_shapes=[
+            pltpu.VMEM((total, GW + width), BF16),
+            pltpu.VMEM((per_pool, total, 2 * hid), F32),
+            pltpu.VMEM((total, per_pool * hid), BF16),
+            pltpu.VMEM((total, width), BF16),
+            pltpu.VMEM((total // 2, width), BF16),
+            pltpu.VMEM((total // 4, width), BF16),
+            pltpu.VMEM((total // 4, width), BF16),
+            pltpu.VMEM((total // 4, width), BF16),
+            pltpu.VMEM((others, PAD, width), BF16),
+            pltpu.VMEM((SLOTS, width // KC, 2 * hid), BF16),
+            pltpu.VMEM((NC, per_pool, hid, width // NC), BF16),
+            pltpu.VMEM((PAD, GW + width), F32),
+            pltpu.VMEM((PAD, width // NC), F32),
+            dma((SLOTS, 2)),
+            dma((NC,)),
+            dma((KC, others)),
+            dma((KC, others)),
+            dma((KC,)),
+            dma((KC,)),
+            dma((KC,)),
+            dma((KC,)),
+            dma((NC,)),
+            dma((NC,)),
+            dma((NC,)),
+            dma((NC,)),
+            dma((NC, others)),
+            dma((NC, others)),
+        ],
+        compiler_params=pltpu.CompilerParams(
+            collective_id=0, has_side_effects=True, vmem_limit_bytes=VMEM_LIMIT
+        ),
+        cost_estimate=pl.CostEstimate(
+            flops=6 * total * width * hid * per_pool,
+            bytes_accessed=6 * width * hid * per_pool,
+            transcendentals=total * hid * per_pool,
+        ),
+    )(hidden_in, norm_gain.reshape(1, width), expert_ids, gate_weights, w_gate, w_up, w_down)
+
+
+VMEM_LIMIT = 63 * 1024 * 1024
+
+
+def body(hidden_in, norm_gain, expert_ids, gate_weights, w_gate, w_up, w_down):
+    batches, rows, width = hidden_in.shape
+    per_pool, _, hid = w_gate.shape
+    small = lax.axis_size("pool") == 4 and lax.axis_size("sub") == 4
+    shaped = batches * rows <= PAD and per_pool == 8 and hid == 384 and width == 4096
+    chosen = kernel_body if small and shaped else dense_body
+    return chosen(hidden_in, norm_gain, expert_ids, gate_weights, w_gate, w_up, w_down)
+
+
 def solution(mesh):
     in_specs = (
         P(None, ("group", "pool", "sub"), None),
@@ -47,4 +359,4 @@
         P("pool", "sub", None),
     )
     out_specs = P(None, ("group", "pool", "sub"), None)
-    return jax.shard_map(dense_body, mesh=mesh, in_specs=in_specs, out_specs=out_specs, check_vma=False)
+    return jax.shard_map(body, mesh=mesh, in_specs=in_specs, out_specs=out_specs, check_vma=False)

time: 176 us -> 71 us (0.40); the launches traced: 173 us -> 70.8 us
  blocking collectives: 87.1 us -> 0 us
  Pallas kernels: 0 us -> 67.9 us
  matrix products: 41.6 us -> 0 us
  between operations: 14.4 us -> 0.01 us
  starting transfers between devices: 11.6 us -> 0 us
  waiting for transfers between devices: 7.84 us -> 0 us
  other arithmetic: 4.68 us -> 0 us
  local copies, waits for them, and re-layouts: 5.87 us -> 2.88 us
    pallas_call x0 -> x1, Pallas kernels: none -> 67.9 us  [kernel_body(): pl.pallas_call(functools.partial(expert_kernel, subs), out_shape=jax.Shap...]
    unnamed x1 -> x0, blocking collectives: 52.5 us -> none
    dot_general x17 -> x0, matrix products: 41.6 us -> none  [the longest x8 17.4 us: dense_body(): gate_act = jnp.dot(rows, w_gate[e], preferred_element_type=jnp.float32)]
    all_gather x1 -> x0, blocking collectives: 34.7 us -> none  [dense_body(): gates = lax.all_gather(gates, ('pool', 'sub'), axis=0, tiled=True)]
    unnamed x4 -> x0, starting transfers between devices: 11.6 us -> none
    all_gather x1 -> x0, waiting for transfers between devices: 7.81 us -> none  [dense_body(): rows = lax.all_gather(normed, ('pool', 'sub'), axis=0, tiled=True)]
    unnamed x25 -> x1, local copies, waits for them, and re-layouts: 5.16 us -> 1.57 us
    convert_element_type x4 -> x0, other arithmetic: 2.46 us -> none  [the longest x2 1.71 us: rms_normed(): return (values * scale * norm_gain.astype(jnp.float32)).astype(jnp.bfloat16)]
  transfers between devices with their start and end apart: 5 -> 0, of which waited for: 1 -> 0; matrix products, arithmetic and copies ran while one was open for 1% -> 0% of each run, Pallas kernels for 0% -> 0%
where the time goes in v1:
time: 71 us; the launch traced here: 70.8 us
  Pallas kernels  67.9 us (96%)
  local copies, waits for them, and re-layouts  2.88 us (4%)
    pallas_call x1, Pallas kernels, kernel_body(): pl.pallas_call(functools.partial(expert_kernel, subs), out_shape=jax.Shap...  67.9 us
    unnamed x1, local copies, waits for them, and re-layouts  1.57 us

profile of v1, /device:TPU:0, one launch (start us, length us, event | category | flops | bytes accessed | tf_op | source)
XLA Modules:
  0.0 70.8 jit_solution(15696317427076511771)
XLA Ops:
  0.0 1.3 %reshape.3.gain = bf16[1,4096]{1,0:T(2,128)(2,1)} reshape(bf16[4096]{0:T(1024)(128)(2,1)} %param.8) | data formatting | bytes 16384 | tf_op jit(solution)/shard_map/reshape | solution.py:336
  1.3 67.9 %shard_map.73 = bf16[3,4,4096]{2,1,0:T(4,128)(2,1)} custom-call(bf16[3,4,4096]{2,1,0:T(4,128)(2,1)} %hidden.1, bf16[1,4096]{1,0:T(2,128)(2,1)} %reshape.3.gain, s32[3,4,8]{2,1,0:T(4,128)} %ids.1, bf16[3,4,8]{2,1,0:T(4,128)(2,1)} %gws.1, bf16[8,4096,384]{2,1,0:T(8,128)(2,1)} %w_gate.1, bf16[8,4096,384]{2,1,0:T(8,128)(2,1)} %w_up.1, bf16[8,384,4096]{2,1,0:T(8,128)(2,1)} %w_down.1), custom_call_target="tpu_custom_call" | custom-call | flops 19327352832 | bytes 75497472 | tf_op jit(solution)/shard_map/pallas_call | solution.py:294
  69.2 1.6 %copy.9 = bf16[3,4,4096]{2,1,0:T(4,128)(2,1)} copy(bf16[3,4,4096]{2,1,0:T(4,128)(2,1)} %shard_map.73) | data formatting | bytes 196608

commit v2 on v1

--- a/solution.py
+++ b/solution.py
@@ -52,7 +52,7 @@
 
 def expert_kernel(
     subs, hidden, gain, ids, gws, w_gate, w_up, w_down, out,
-    xg, acc, act, y, crecv, xsend, xrecv, zsend, zrecv, gu, wd, rowf, sumf,
+    xg, xc, acc, act, y, crecv, xsend, xrecv, zsend, zrecv, gu, wd, rowf, sumf, packer_ref, padder_ref,
     gu_sem, wd_sem, az_s, az_r, ax_s, ax_r, ac_s, ac_r,
     rc_s, rc_r, rx_s, rx_r, rz_s, rz_r,
 ):
@@ -61,8 +61,12 @@
     kw, nw = width // KC, width // NC
     group, pool, sub = lax.axis_index("group"), lax.axis_index("pool"), lax.axis_index("sub")
     core, side = pool % 2, pool // 2
+    block = batches * rows
     quad = subs * PAD
     half = 2 * quad
+    cquad = subs * block
+    chalf = 2 * cquad
+    ctotal = 2 * chalf
     xrow = core * half + side * quad
     own = pl.multiple_of(xrow + sub * PAD, PAD)
     peer_core = (group, side * 2 + 1 - core, sub)
@@ -150,21 +154,34 @@
     relay_x(0)
     relay_x(1)
     relay_c(0)
+    relay_x(2)
+
+    source = lax.broadcasted_iota(jnp.int32, (ctotal, 2 * half), 1)
+    target = lax.broadcasted_iota(jnp.int32, (ctotal, 2 * half), 0)
+    inside = source & (PAD - 1)
+    packer = ((target == (source >> 4) * block + inside) & (inside < block)).astype(F32).astype(BF16)
+    source = lax.broadcasted_iota(jnp.int32, (quad, cquad), 1)
+    target = lax.broadcasted_iota(jnp.int32, (quad, cquad), 0)
+    inside = target & (PAD - 1)
+    padder_ref[...] = (
+        ((source == (target >> 4) * block + inside) & (inside < block)).astype(F32).astype(BF16)
+    )
+    packer_ref[...] = packer
 
     def gu_step(c, step, carry):
         slot, e = step % SLOTS, step % per_pool
         for copy in gu_copies(step):
             copy.wait()
         total = acc[e] + jnp.dot(
-            xg[:, GW + c * kw : GW + (c + 1) * kw], gu[slot], preferred_element_type=F32
+            xc[:, GW + c * kw : GW + (c + 1) * kw], gu[slot], preferred_element_type=F32
         )
         if c < KC - 1:
             acc[e] = total
         else:
             g, u = total[:, :hid], total[:, hid:]
-            lanes = lax.broadcasted_iota(jnp.int32, (2 * half, GW), 1)
+            lanes = lax.broadcasted_iota(jnp.int32, (ctotal, GW), 1)
             weight = jnp.sum(
-                jnp.where(lanes == pool * per_pool + e, xg[:, :GW].astype(F32), 0.0), axis=1, keepdims=True
+                jnp.where(lanes == pool * per_pool + e, xc[:, :GW].astype(F32), 0.0), axis=1, keepdims=True
             )
             act[:, pl.ds(pl.multiple_of(e * hid, hid), hid)] = (
                 g / (1.0 + jnp.exp(-g)) * u * weight
@@ -186,10 +203,15 @@
     cut = per_pool // 2
     for c in range(KC):
         ac(c).wait_recv()
+        low = 0 if c == 0 else GW + c * kw
+        high = GW + (c + 1) * kw
+        xc[:, low:high] = jnp.dot(
+            packer_ref[...], xg[:, low:high], preferred_element_type=F32
+        ).astype(BF16)
         base = c * per_pool
         lax.fori_loop(base, base + cut, functools.partial(gu_step, c), 0)
-        if c + 2 < KC:
-            relay_x(c + 2)
+        if c + 3 < KC:
+            relay_x(c + 3)
         if c + 1 < KC:
             relay_c(c + 1)
         lax.fori_loop(base + cut, base + per_pool, functools.partial(gu_step, c), 0)
@@ -199,7 +221,7 @@
 
     def rc(n):
         return pltpu.make_async_remote_copy(
-            y.at[pl.ds(pl.multiple_of((1 - core) * half, PAD), half), ncols(n)], crecv.at[:, ncols(n)],
+            y.at[pl.ds(pl.multiple_of((1 - core) * chalf, PAD), chalf), ncols(n)], crecv.at[:, ncols(n)],
             rc_s.at[n], rc_r.at[n], device_id=peer_core, device_id_type=MESH,
         )
 
@@ -229,29 +251,32 @@
         def _():
             m = n - 1
             rc(m).wait_recv()
-            far = pl.multiple_of((1 - side) * quad, PAD)
+            far = pl.multiple_of((1 - side) * cquad, PAD)
             xsend[:, ncols(m)] = (
-                y[pl.ds(pl.multiple_of(core * half + (1 - side) * quad, PAD), quad), ncols(m)].astype(F32)
-                + crecv[pl.ds(far, quad), ncols(m)].astype(F32)
+                y[pl.ds(pl.multiple_of(core * chalf + (1 - side) * cquad, PAD), cquad), ncols(m)].astype(F32)
+                + crecv[pl.ds(far, cquad), ncols(m)].astype(F32)
             ).astype(BF16)
             rx(m).start()
 
-        @pl.when((n >= 2) & (n < NC + 2))
-        def _():
-            m = n - 2
+        @pl.when((n >= 3) & (n < NC + 3))
+        def _():
+            m = n - 3
             rx(m).wait_recv()
-            near = pl.multiple_of(side * quad, PAD)
-            zsend[:, ncols(m)] = (
-                y[pl.ds(pl.multiple_of(xrow, PAD), quad), ncols(m)].astype(F32)
-                + crecv[pl.ds(near, quad), ncols(m)].astype(F32)
+            near = pl.multiple_of(side * cquad, PAD)
+            chosen = (
+                y[pl.ds(pl.multiple_of(core * chalf + side * cquad, PAD), cquad), ncols(m)].astype(F32)
+                + crecv[pl.ds(near, cquad), ncols(m)].astype(F32)
                 + xrecv[:, ncols(m)].astype(F32)
+            ).astype(BF16)
+            zsend[:, ncols(m)] = jnp.dot(
+                padder_ref[...], chosen, preferred_element_type=F32
             ).astype(BF16)
             for d in range(subs - 1):
                 rz(m, d).start()
 
-        @pl.when(n >= 3)
-        def _():
-            m = n - 3
+        @pl.when(n >= 5)
+        def _():
+            m = n - 5
             total = zsend[pl.ds(pl.multiple_of(sub * PAD, PAD), PAD), ncols(m)].astype(F32)
             for d in range(subs - 1):
                 rz(m, d).wait_recv()
@@ -264,7 +289,7 @@
 
         return carry
 
-    lax.fori_loop(0, NC + 3, down_step, 0)
+    lax.fori_loop(0, NC + 5, down_step, 0)
 
     for c in range(KC):
         for d in range(subs - 1):
@@ -287,6 +312,7 @@
     per_pool, _, hid = w_gate.shape
     subs = lax.axis_size("sub")
     total = 4 * subs * PAD
+    ctotal = 4 * subs * batches * rows
     vmem = pl.BlockSpec(memory_space=pltpu.VMEM)
     hbm = pl.BlockSpec(memory_space=pl.ANY)
     dma = pltpu.SemaphoreType.DMA
@@ -298,18 +324,21 @@
         out_specs=vmem,
         scratch_shapes=[
             pltpu.VMEM((total, GW + width), BF16),
-            pltpu.VMEM((per_pool, total, 2 * hid), F32),
-            pltpu.VMEM((total, per_pool * hid), BF16),
-            pltpu.VMEM((total, width), BF16),
-            pltpu.VMEM((total // 2, width), BF16),
-            pltpu.VMEM((total // 4, width), BF16),
-            pltpu.VMEM((total // 4, width), BF16),
+            pltpu.VMEM((ctotal, GW + width), BF16),
+            pltpu.VMEM((per_pool, ctotal, 2 * hid), F32),
+            pltpu.VMEM((ctotal, per_pool * hid), BF16),
+            pltpu.VMEM((ctotal, width), BF16),
+            pltpu.VMEM((ctotal // 2, width), BF16),
+            pltpu.VMEM((ctotal // 4, width), BF16),
+            pltpu.VMEM((ctotal // 4, width), BF16),
             pltpu.VMEM((total // 4, width), BF16),
             pltpu.VMEM((others, PAD, width), BF16),
             pltpu.VMEM((SLOTS, width // KC, 2 * hid), BF16),
             pltpu.VMEM((NC, per_pool, hid, width // NC), BF16),
             pltpu.VMEM((PAD, GW + width), F32),
             pltpu.VMEM((PAD, width // NC), F32),
+            pltpu.VMEM((ctotal, total), BF16),
+            pltpu.VMEM((total // 4, ctotal // 4), BF16),
             dma((SLOTS, 2)),
             dma((NC,)),
             dma((KC, others)),
@@ -343,7 +372,7 @@
     batches, rows, width = hidden_in.shape
     per_pool, _, hid = w_gate.shape
     small = lax.axis_size("pool") == 4 and lax.axis_size("sub") == 4
-    shaped = batches * rows <= PAD and per_pool == 8 and hid == 384 and width == 4096
+    shaped = batches * rows == 12 and per_pool == 8 and hid == 384 and width == 4096
     chosen = kernel_body if small and shaped else dense_body
     return chosen(hidden_in, norm_gain, expert_ids, gate_weights, w_gate, w_up, w_down)
 

time: 71 us -> 62.3 us (0.88)
  Pallas kernels: 67.9 us -> 59.2 us
    pallas_call x1, Pallas kernels: 67.9 us -> 59.2 us  [kernel_body(): pl.pallas_call(functools.partial(expert_kernel, subs), out_shape=jax.Shap...]
where the time goes in v2:
time: 62.3 us; the launch traced here: 62.1 us
  Pallas kernels  59.2 us (95%)
  local copies, waits for them, and re-layouts  2.88 us (5%)
    pallas_call x1, Pallas kernels, kernel_body(): pl.pallas_call(functools.partial(expert_kernel, subs), out_shape=jax.Shap...  59.2 us
    unnamed x1, local copies, waits for them, and re-layouts  1.57 us
    reshape x1, local copies, waits for them, and re-layouts, kernel_body(): norm_gain.reshape(1, width)  1.31 us

profile of v2, /device:TPU:0, one launch (start us, length us, event | category | flops | bytes accessed | tf_op | source)
XLA Modules:
  0.0 62.1 jit_solution(5853197325505107838)
XLA Ops:
  0.0 1.3 %reshape.3.gain = bf16[1,4096]{1,0:T(2,128)(2,1)} reshape(bf16[4096]{0:T(1024)(128)(2,1)} %param.8) | data formatting | bytes 16384 | tf_op jit(solution)/shard_map/reshape | solution.py:365
  1.3 59.2 %shard_map.73 = bf16[3,4,4096]{2,1,0:T(4,128)(2,1)} custom-call(bf16[3,4,4096]{2,1,0:T(4,128)(2,1)} %hidden.1, bf16[1,4096]{1,0:T(2,128)(2,1)} %reshape.3.gain, s32[3,4,8]{2,1,0:T(4,128)} %ids.1, bf16[3,4,8]{2,1,0:T(4,128)(2,1)} %gws.1, bf16[8,4096,384]{2,1,0:T(8,128)(2,1)} %w_gate.1, bf16[8,4096,384]{2,1,0:T(8,128)(2,1)} %w_up.1, bf16[8,384,4096]{2,1,0:T(8,128)(2,1)} %w_down.1), custom_call_target="tpu_custom_call" | custom-call | flops 19327352832 | bytes 75497472 | tf_op jit(solution)/shard_map/pallas_call | solution.py:320
  60.5 1.6 %copy.9 = bf16[3,4,4096]{2,1,0:T(4,128)(2,1)} copy(bf16[3,4,4096]{2,1,0:T(4,128)(2,1)} %shard_map.73) | data formatting | bytes 196608
